TPU v7x, 32 devices: a whole 2x2x4 slice. The times are simulated.
32 devices in a mesh: px: 8 (over z, y), py: 4 (over x, core).
Axes of the slice: x: 2, y: 2, z: 4, core: 2. Of those that a mesh axis runs over, the one named last changes fastest.
Arguments:
- right_sides: bfloat16 [16, 2048, 512], P('px', 'py'), may hold values from -6 to 6
- tree_order: int32 [16, 2048], P('px', 'py'), may hold values from 0 to 2047, as said below
- dense_blocks: bfloat16 [16, 2048, 2048], P('px', 'py'), may hold values from -0.125 to 0.125
- basis_out: bfloat16 [16, 2048, 256], P('px', 'py'), may hold values from -0.375 to 0.375
- basis_in: bfloat16 [16, 2048, 256], P('px', 'py'), may hold values from -0.125 to 0.125
- leaf_transfer: bfloat16 [16, 256, 256], P('px'), may hold values from -0.375 to 0.375
- leaf_coupling: bfloat16 [16, 256, 256], P('px'), may hold values from -0.09375 to 0.09375
- chain_transfer: bfloat16 [8, 3, 256, 256], P('px'), as said below
- chain_coupling: bfloat16 [8, 3, 256, 256], P('px'), as said below
Outputs:
- kernel_product: float32 [16, 2048, 512], P('px', 'py')
Inputs may be any that keep to these rules, and one draw needn't show every extreme that they name: `tree_order`: each row is a permutation, and each aligned block of 512 entries holds exactly the positions of that block. `chain_transfer`: entry [p, k] is the same matrix for all p with the same p // 2**k. `chain_coupling`: entry [p, k] is the same matrix for all p with the same p // 2**k.
All inputs are finite; a program needn't handle non-finite values.
Results may differ from a plain program's by a relative error of at most 0.0019.
Values may be sent and summed in bfloat16 or wider, within the bound.
A program may use at most 64 MiB of HBM per device.

v0:
```python
import jax
import jax.numpy as jnp
from jax import lax
from jax.sharding import PartitionSpec as P

HIGHEST = lax.Precision.HIGHEST


def partner(value, axis, distance):
    mask = 2**distance
    pairs = [(source, source ^ mask) for source in range(lax.axis_size(axis))]
    return lax.ppermute(value, axis, pairs)


def lift(weight, values):
    return jnp.dot(weight.astype(jnp.float32).T, values, precision=HIGHEST)


def lower(weight, values):
    return jnp.dot(weight.astype(jnp.float32), values, precision=HIGHEST)


def pick_rows(values, indices):
    return values[indices]


def place_rows(values, indices):
    return jnp.zeros_like(values).at[indices].set(values)


def on_device(
    right_sides,
    tree_order,
    dense_blocks,
    basis_out,
    basis_in,
    leaf_transfer,
    leaf_coupling,
    chain_transfer,
    chain_coupling,
):
    row_count = tree_order.shape[1]
    width = right_sides.shape[2]
    rank = basis_in.shape[2]
    levels = lax.axis_size("px").bit_length() - 1
    positions = tree_order - lax.axis_index("py") * row_count
    permuted = jax.vmap(pick_rows)(right_sides, positions)
    nearby = jnp.einsum(
        "npk,nkr->npr",
        dense_blocks,
        lax.all_gather(permuted, "py", axis=1, tiled=True),
        preferred_element_type=jnp.float32,
    )
    coefficients = jnp.einsum(
        "npk,npr->nkr", basis_in, permuted, preferred_element_type=jnp.float32
    )
    coefficients = lax.psum(coefficients, "py")
    subtree = lift(leaf_transfer[0], coefficients[0]) + lift(leaf_transfer[1], coefficients[1])
    gathered = []
    for height in range(levels):
        contrib = lift(chain_transfer[0, height], subtree)
        other_subtree, other_contrib = partner((subtree, contrib), "px", height)
        gathered.append(other_subtree)
        subtree = contrib + other_contrib
    others = jnp.stack(gathered)
    descend = jnp.zeros((rank, width), jnp.float32)
    for height in reversed(range(levels)):
        descend = lower(chain_coupling[0, height], others[height]) + lower(
            chain_transfer[0, height], descend
        )
    first_down = lower(leaf_coupling[0], coefficients[1]) + lower(leaf_transfer[0], descend)
    second_down = lower(leaf_coupling[1], coefficients[0]) + lower(leaf_transfer[1], descend)
    leaf_down = jnp.stack([first_down, second_down]).astype(jnp.bfloat16)
    distant = jnp.einsum("npk,nkr->npr", basis_out, leaf_down, preferred_element_type=jnp.float32)
    return jax.vmap(place_rows)(nearby + distant, positions)


def solution(mesh):
    in_specs = (
        P("px", "py", None),
        P("px", "py"),
        P("px", "py", None),
        P("px", "py", None),
        P("px", "py", None),
        P("px", None, None),
        P("px", None, None),
        P("px", None, None, None),
        P("px", None, None, None),
    )
    out_specs = P("px", "py", None)
    return jax.shard_map(
        on_device, mesh=mesh, in_specs=in_specs, out_specs=out_specs, check_vma=False
    )
```

profile of v0, /device:TPU:0, one launch (start us, length us, event | category | flops | bytes accessed | tf_op | source)
XLA Modules:
  0.0 133.8 jit_solution(7353619527105987406)
XLA Ops:
  6.5 0.0 copy-start
  6.5 0.0 all-reduce.2.cloned.1.call-start
  6.5 0.8 or_bitcast_fusion
  7.3 0.4 copy-done
  7.8 0.0 copy-start.6
  7.8 7.3 %gather_fusion = bf16[1024,512]{1,0:T(8,128)(2,1)S(1)} fusion(bf16[2,512,512]{2,1,0:T(8,128)(2,1)S(1)} %copy-done, s32[1024]{0:T(1024)S(1)} %bitcast.90), kind=kCustom, calls=%fused_computation | custom fusion | bytes 2105344 | tf_op jit(solution)/shard_map/vmap()/gather | solution.py:24
  15.1 0.0 copy-start.1
  15.1 0.0 copy-done.6
  15.1 0.0 copy-start.5
  15.1 1.5 %convolution_bitcast_fusion = f32[2,256,512]{1,2,0:T(8,128)} fusion(bf16[2,512,512]{2,1,0:T(8,128)(2,1)S(1)} %bitcast.91, bf16[2,512,256]{2,1,0:T(8,128)(2,1)S(1)} %copy-done.6), kind=kOutput, calls=%fused_computation.3 | convolution fusion | flops 268435456 | bytes 2621440 | tf_op jit(solution)/shard_map/npk,npr->nkr/dot_general | solution.py:54
  16.7 0.0 all-reduce.2.cloned.1.call-update
  16.7 0.0 copy-start.3
  16.7 0.0 all-gather.2.cloned.1.call-start
  16.7 0.0 copy-done.1
  16.7 0.7 all-gather.2.cloned.1.call-update
  17.4 38.1 %all-reduce.2.cloned.1.call-done = f32[2,256,512]{1,2,0:T(8,128)} async-done(((f32[2,256,512]{1,2,0:T(8,128)}), f32[2,256,512]{1,2,0:T(8,128)}) %all-reduce.2.cloned.1.call-update) | async-done | bytes 1048592 | tf_op jit(solution)/shard_map/psum | solution.py:57
  55.6 0.0 copy-done.5
  55.6 1.4 %fusion.11 = f32[512,256]{1,0:T(8,128)S(1)} fusion(f32[2,256,512]{1,2,0:T(8,128)} %all-reduce.2.cloned.1.call-done, bf16[2,256,256]{2,1,0:T(8,128)(2,1)S(1)} %copy-done.5), kind=kOutput, calls=%fused_computation.25 | convolution fusion | flops 402653184 | bytes 1179648 | tf_op jit(solution)/shard_map/dot_general | solution.py:16
  57.0 1.4 %convolution_add_fusion.6 = f32[512,256]{1,0:T(8,128)S(1)} fusion(f32[512,256]{1,0:T(8,128)S(1)} %fusion.11, f32[2,256,512]{1,2,0:T(8,128)} %all-reduce.2.cloned.1.call-done, bf16[2,256,256]{2,1,0:T(8,128)(2,1)S(1)} %copy-done.5), kind=kOutput, calls=%fused_computation.11 | convolution fusion | flops 402784256 | bytes 1703936 | tf_op jit(solution)/shard_map/dot_general | solution.py:16
  58.4 0.0 copy-done.3
  58.5 0.0 copy-start.10
  58.5 0.0 copy-start.11
  58.5 0.4 convolution_bitcast_fusion.2
  58.9 1.5 %collective-permute-start.1 = (f32[256,512]{0,1:T(8,128)S(1)}, f32[256,512]{0,1:T(8,128)S(1)}, u32[]{:S(2)}, u32[]{:S(2)}) collective-permute-start(f32[256,512]{0,1:T(8,128)S(1)} %convolution_bitcast_fusion.2), channel_id=1, source_target_pairs={{0,4},{4,0},{8,12},{12,8},{16,20},{20,16},{24,28},{28,24},{1,5},{5... | collective-permute-start | bytes 1572872 | tf_op jit(solution)/shard_map/ppermute | solution.py:12
  60.4 12.0 %collective-permute-done.1 = f32[256,512]{0,1:T(8,128)S(1)} collective-permute-done((f32[256,512]{0,1:T(8,128)S(1)}, f32[256,512]{0,1:T(8,128)S(1)}, u32[]{:S(2)}, u32[]{:S(2)}) %collective-permute-start.1) | collective-permute-done | bytes 524320 | tf_op jit(solution)/shard_map/ppermute | solution.py:12
  72.4 0.1 add.51
  72.5 0.0 copy-start.2
  72.5 0.0 copy-start.9
  72.5 0.4 convolution_bitcast_fusion.1
  72.9 1.3 collective-permute-start.3
  74.2 0.0 copy-done.10
  74.2 0.1 multiply_reduce_fusion
  74.3 0.0 copy-done.11
  74.3 0.1 and_reduce_fusion
  74.4 0.4 fusion.12
  74.8 0.0 copy-start.8
  74.8 10.8 %collective-permute-done.3 = f32[256,512]{0,1:T(8,128)S(1)} collective-permute-done((f32[256,512]{0,1:T(8,128)S(1)}, f32[256,512]{0,1:T(8,128)S(1)}, u32[]{:S(2)}, u32[]{:S(2)}) %collective-permute-start.3) | collective-permute-done | bytes 524320 | tf_op jit(solution)/shard_map/ppermute | solution.py:12
  85.6 0.1 add.52
  85.7 2.0 %collective-permute-start.4 = (f32[256,512]{0,1:T(8,128)S(1)}, f32[256,512]{0,1:T(8,128)S(1)}, u32[]{:S(2)}, u32[]{:S(2)}) collective-permute-start(f32[256,512]{0,1:T(8,128)S(1)} %add.52), channel_id=1, source_target_pairs={{0,16},{4,20},{8,24},{12,28},{16,0},{20,4},{24,8},{28,12},{1,17},{... | collective-permute-start | bytes 1572872 | tf_op jit(solution)/shard_map/ppermute | solution.py:12
  87.6 1.5 %collective-permute-start = (f32[256,512]{0,1:T(8,128)S(1)}, f32[256,512]{0,1:T(8,128)S(1)}, u32[]{:S(2)}, u32[]{:S(2)}) collective-permute-start(f32[256,512]{0,1:T(8,128)S(1)} %bitcast.94), channel_id=1, source_target_pairs={{0,4},{4,0},{8,12},{12,8},{16,20},{20,16},{24,28},{28,24},{1,5},{5... | collective-permute-start | bytes 1572872 | tf_op jit(solution)/shard_map/ppermute | solution.py:12
  89.1 0.0 copy-done.2
  89.1 0.0 copy-done.9
  89.1 0.4 fusion.9
  89.5 1.6 %collective-permute-start.2 = (f32[256,512]{0,1:T(8,128)S(1)}, f32[256,512]{0,1:T(8,128)S(1)}, u32[]{:S(2)}, u32[]{:S(2)}) collective-permute-start(f32[256,512]{0,1:T(8,128)S(1)} %add.51), channel_id=1, source_target_pairs={{0,8},{4,12},{8,0},{12,4},{16,24},{20,28},{24,16},{28,20},{1,9},{5... | collective-permute-start | bytes 1572872 | tf_op jit(solution)/shard_map/ppermute | solution.py:12
  91.1 0.4 fusion.10
  91.5 18.3 %collective-permute-done.4 = f32[256,512]{0,1:T(8,128)S(1)} collective-permute-done((f32[256,512]{0,1:T(8,128)S(1)}, f32[256,512]{0,1:T(8,128)S(1)}, u32[]{:S(2)}, u32[]{:S(2)}) %collective-permute-start.4) | collective-permute-done | bytes 524320 | tf_op jit(solution)/shard_map/ppermute | solution.py:12
  109.8 0.0 copy-done.8
  109.8 0.4 convolution_add_fusion.3
  110.2 0.4 fusion.17
  110.6 0.9 collective-permute-done.2
  111.6 0.4 convolution_add_fusion.4
  112.0 0.4 fusion.21
  112.4 0.0 collective-permute-done
  112.4 0.4 convolution_add_fusion.5
  112.9 0.4 fusion.3
  113.3 1.1 fusion.2
  114.4 0.0 all-gather.2.cloned.1.call-done
  114.4 0.0 copy-start.4
  114.4 0.0 copy-start.7
  114.4 5.8 %fusion.48 = f32[2,512,512]{1,2,0:T(8,128)S(1)} fusion(bf16[2,512,2048]{2,1,0:T(8,128)(2,1)} %param.11, bf16[2,2048,512]{2,1,0:T(8,128)(2,1)} %all-gather.2.cloned.1.call-done), kind=kOutput, calls=%fused_computation.67 | convolution fusion | flops 2147483648 | bytes 10485760 | tf_op jit(solution)/shard_map/npk,nkr->npr/dot_general | solution.py:48
  120.3 0.0 copy-done.4
  120.3 0.0 copy-done.7
  120.3 0.5 convolution_add_fusion
  120.8 6.2 %scatter_custom_fusion = f32[1024,512]{1,0:T(8,128)} fusion(s32[1024]{0:T(1024)S(1)} %bitcast.95, f32[1024,512]{1,0:T(8,128)S(1)} %bitcast.93, f32[]{:T(128)} %constant.4.clone.1), kind=kCustom, calls=%fused_computation.16 | custom fusion | bytes 2097156
  (4 shorter events, 0.0 us)
Async XLA Ops:
  6.5 1.2 copy-start
  6.5 49.1 %all-reduce.2.cloned.1.call-start = ((), (), s32[]{:S(2)}) async-start(), calls=%async_computation.1 | async-start | bytes 2097152 | tf_op jit(solution)/shard_map/psum | solution.py:57
  7.8 7.3 %copy-start.6 = (bf16[2,512,256]{2,1,0:T(8,128)(2,1)S(1)}, bf16[2,512,256]{2,1,0:T(8,128)(2,1)}, u32[]{:S(2)}) copy-start(bf16[2,512,256]{2,1,0:T(8,128)(2,1)} %param.13) | copy-start | bytes 1572868
  15.1 1.7 %copy-start.1 = (bf16[1024,512]{1,0:T(8,128)(2,1)}, bf16[1024,512]{1,0:T(8,128)(2,1)S(1)}, u32[]{:S(2)}) copy-start(bf16[1024,512]{1,0:T(8,128)(2,1)S(1)} %gather_fusion) | copy-start | bytes 3145732
  15.1 40.5 %copy-start.5 = (bf16[2,256,256]{2,1,0:T(8,128)(2,1)S(1)}, bf16[2,256,256]{2,1,0:T(8,128)(2,1)}, u32[]{:S(2)}) copy-start(bf16[2,256,256]{2,1,0:T(8,128)(2,1)} %param.14) | copy-start | bytes 786436
  16.7 41.8 %copy-start.3 = (bf16[1,3,256,256]{3,2,1,0:T(8,128)(2,1)S(1)}, bf16[1,3,256,256]{3,2,1,0:T(8,128)(2,1)}, u32[]{:S(2)}) copy-start(bf16[1,3,256,256]{3,2,1,0:T(8,128)(2,1)} %param.16) | copy-start | bytes 1179652
  16.7 97.7 %all-gather.2.cloned.1.call-start = ((), (), s32[]{:S(2)}) async-start(), calls=%async_computation | async-start | bytes 5242880 | tf_op jit(solution)/shard_map/all_gather | solution.py:51
  58.5 15.7 %copy-start.10 = (s32[2]{0:T(128)S(1)}, s32[2]{0:T(128)}, u32[]{:S(2)}) copy-start(s32[2]{0:T(128)} %constant.21) | copy-start | bytes 28
  58.5 15.8 %copy-start.11 = (s32[2]{0:T(128)S(1)}, s32[2]{0:T(128)}, u32[]{:S(2)}) copy-start(s32[2]{0:T(128)} %constant.24) | copy-start | bytes 28
  58.9 13.5 %collective-permute-start.1 = (f32[256,512]{0,1:T(8,128)S(1)}, f32[256,512]{0,1:T(8,128)S(1)}, u32[]{:S(2)}, u32[]{:S(2)}) collective-permute-start(f32[256,512]{0,1:T(8,128)S(1)} %convolution_bitcast_fusion.2), channel_id=1, source_target_pairs={{0,4},{4,0},{8,12},{12,8},{16,20},{20,16},{24,28},{28,24},{1,5},{5... | collective-permute-start | bytes 1572872 | tf_op jit(solution)/shard_map/ppermute | solution.py:12
  72.5 16.6 %copy-start.2 = (f32[2,256,512]{1,2,0:T(8,128)S(1)}, f32[2,256,512]{1,2,0:T(8,128)}, u32[]{:S(2)}) copy-start(f32[2,256,512]{1,2,0:T(8,128)} %all-reduce.2.cloned.1.call-done) | copy-start | bytes 3145732
  72.5 16.6 %copy-start.9 = (bf16[2,256,256]{2,1,0:T(8,128)(2,1)S(1)}, bf16[2,256,256]{2,1,0:T(8,128)(2,1)}, u32[]{:S(2)}) copy-start(bf16[2,256,256]{2,1,0:T(8,128)(2,1)} %param.15) | copy-start | bytes 786436
  72.9 12.7 %collective-permute-start.3 = (f32[256,512]{0,1:T(8,128)S(1)}, f32[256,512]{0,1:T(8,128)S(1)}, u32[]{:S(2)}, u32[]{:S(2)}) collective-permute-start(f32[256,512]{0,1:T(8,128)S(1)} %convolution_bitcast_fusion.1), channel_id=1, source_target_pairs={{0,8},{4,12},{8,0},{12,4},{16,24},{20,28},{24,16},{28,20},{1,9},{5... | collective-permute-start | bytes 1572872 | tf_op jit(solution)/shard_map/ppermute | solution.py:12
  74.8 35.0 %copy-start.8 = (bf16[1,3,256,256]{3,2,1,0:T(8,128)(2,1)S(1)}, bf16[1,3,256,256]{3,2,1,0:T(8,128)(2,1)}, u32[]{:S(2)}) copy-start(bf16[1,3,256,256]{3,2,1,0:T(8,128)(2,1)} %param.17) | copy-start | bytes 1179652
  85.7 24.1 %collective-permute-start.4 = (f32[256,512]{0,1:T(8,128)S(1)}, f32[256,512]{0,1:T(8,128)S(1)}, u32[]{:S(2)}, u32[]{:S(2)}) collective-permute-start(f32[256,512]{0,1:T(8,128)S(1)} %add.52), channel_id=1, source_target_pairs={{0,16},{4,20},{8,24},{12,28},{16,0},{20,4},{24,8},{28,12},{1,17},{... | collective-permute-start | bytes 1572872 | tf_op jit(solution)/shard_map/ppermute | solution.py:12
  87.6 24.8 %collective-permute-start = (f32[256,512]{0,1:T(8,128)S(1)}, f32[256,512]{0,1:T(8,128)S(1)}, u32[]{:S(2)}, u32[]{:S(2)}) collective-permute-start(f32[256,512]{0,1:T(8,128)S(1)} %bitcast.94), channel_id=1, source_target_pairs={{0,4},{4,0},{8,12},{12,8},{16,20},{20,16},{24,28},{28,24},{1,5},{5... | collective-permute-start | bytes 1572872 | tf_op jit(solution)/shard_map/ppermute | solution.py:12
  89.5 22.0 %collective-permute-start.2 = (f32[256,512]{0,1:T(8,128)S(1)}, f32[256,512]{0,1:T(8,128)S(1)}, u32[]{:S(2)}, u32[]{:S(2)}) collective-permute-start(f32[256,512]{0,1:T(8,128)S(1)} %add.51), channel_id=1, source_target_pairs={{0,8},{4,12},{8,0},{12,4},{16,24},{20,28},{24,16},{28,20},{1,9},{5... | collective-permute-start | bytes 1572872 | tf_op jit(solution)/shard_map/ppermute | solution.py:12
  114.4 5.9 %copy-start.4 = (bf16[1,256,512]{1,2,0:T(8,128)(2,1)S(1)}, bf16[1,256,512]{1,2,0:T(8,128)(2,1)}, u32[]{:S(2)}) copy-start(bf16[1,256,512]{1,2,0:T(8,128)(2,1)} %fusion.2) | copy-start | bytes 786436
  114.4 5.9 %copy-start.7 = (bf16[2,512,256]{2,1,0:T(8,128)(2,1)S(1)}, bf16[2,512,256]{2,1,0:T(8,128)(2,1)}, u32[]{:S(2)}) copy-start(bf16[2,512,256]{2,1,0:T(8,128)(2,1)} %param.12) | copy-start | bytes 1572868
Sparse Core Ops, SparseCore 0:
  16.8 38.7 all-reduce.1
  57.2 34.8 all-gather.1
where the time goes:
time: 134 us
  waiting for transfers between devices  80.8 us (60%)
  matrix products  16.3 us (12%)
  local copies, waits for them, and re-layouts  14 us (10%)
  between operations  13.6 us (10%)
  starting transfers between devices  7.88 us (6%)
    ppermute x5, waiting for transfers between devices, partner(): return lax.ppermute(value, axis, pairs)  42 us
    psum x1, waiting for transfers between devices, on_device(): coefficients = lax.psum(coefficients, 'py')  38.1 us
    ppermute x5, starting transfers between devices, partner(): return lax.ppermute(value, axis, pairs)  7.84 us
    gather x1, local copies, waits for them, and re-layouts, pick_rows(): return values[indices]  7.29 us
    unnamed x27, local copies, waits for them, and re-layouts  6.72 us
    dot_general x1, matrix products, on_device(): jnp.einsum('npk,nkr->npr', dense_blocks, lax.all_gather(permuted, 'py', a...  5.85 us
    dot_general x10, matrix products, lower(): return jnp.dot(weight.astype(jnp.float32), values, precision=HIGHEST)  4.86 us
    dot_general x4, matrix products, lift(): return jnp.dot(weight.astype(jnp.float32).T, values, precision=HIGHEST)  3.62 us
  transfers between devices with their start and end apart: 7, of which 5 were waited for; matrix products, arithmetic and copies ran while one was open for 7% of the time, Pallas kernels for 0%

commit v1 on v0

v1 whole, which is shorter than its diff:
```python
import functools

import jax
import jax.numpy as jnp
from jax import lax
from jax.experimental import pallas as pl
from jax.experimental.pallas import tpu as pltpu
from jax.sharding import PartitionSpec as P

MESH = pl.DeviceIdType.MESH
BF16 = jnp.bfloat16
F32 = jnp.float32
CHUNKS = 4


def dot(a, b):
    return jnp.dot(a, b, preferred_element_type=F32)


def dot_nt(a, b):
    return lax.dot_general(a, b, (((1,), (1,)), ((), ())), preferred_element_type=F32)


def dot_tn(a, b):
    return lax.dot_general(a, b, (((0,), (0,)), ((), ())), preferred_element_type=F32)


def halves(v):
    high = v.astype(BF16)
    low = (v - high.astype(F32)).astype(BF16)
    return jnp.concatenate([high, low], axis=0)


def lift(v, w):
    t = dot(halves(v), w)
    n = v.shape[0]
    return t[:n] + t[n:]


def lower(v, w):
    t = dot_nt(halves(v), w)
    n = v.shape[0]
    return t[:n] + t[n:]


def kernel(
    npx,
    npy,
    rs_in,
    order,
    dense_in,
    bout_in,
    bin_in,
    lt_in,
    lc_in,
    ct_in,
    cc_in,
    out,
    rs,
    dense,
    bout,
    bin_,
    lt,
    lc,
    ct,
    cc,
    onehot,
    moved,
    bmoved,
    coef,
    near_in,
    part,
    far_in,
    g,
    near,
    wsib,
    ssend,
    srecv,
    ldg,
    result,
    load_sem,
    out_sem,
    w_sem,
    near_sem,
    far_sem,
    own_sem,
    x_sem,
    fwd_sem,
    s_sem,
    ld_sem,
    ldf_sem,
):
    levels = npx.bit_length() - 1
    nx = npy // 2
    leaves, rows, width = rs.shape
    n = width // npy
    px = lax.axis_index("px")
    py = lax.axis_index("py")
    x = py // 2
    c = py % 2
    twin = {"py": 2 * x + 1 - c}

    def chip(d):
        return lax.rem(x + d + nx, nx)

    def peer(d):
        return {"py": 2 * chip(d) + c}

    def sibling(k):
        bit = (px // 2**k) % 2
        return {"px": px + 2**k * (1 - 2 * bit)}

    def remote(src, dst, sems, index, device):
        return pltpu.make_async_remote_copy(
            src_ref=src,
            dst_ref=dst,
            send_sem=sems.at[(0,) + index],
            recv_sem=sems.at[(1,) + index],
            device_id=device,
            device_id_type=MESH,
        )

    loads = []

    def load(src, dst):
        copy = pltpu.make_async_copy(src, dst, load_sem.at[len(loads)])
        copy.start()
        loads.append(copy)
        return copy

    early = [load(bin_in, bin_), load(rs_in, rs)]
    tree_loads = [load(lt_in, lt), load(ct_in, ct), load(lc_in, lc), load(cc_in, cc)]
    bout_load = load(bout_in, bout)
    dense_loads = [
        [load(dense_in.at[l, :, pl.ds(q * rows, rows)], dense.at[l, q]) for q in range(npy)]
        for l in range(leaves)
    ]

    partners = [twin] + [peer(d) for d in range(1, nx)] + [sibling(k) for k in range(levels)]
    barrier = pltpu.get_barrier_semaphore()
    for device in partners:
        pl.semaphore_signal(barrier, inc=1, device_id=device, device_id_type=MESH)
    pl.semaphore_wait(barrier, len(partners))

    w_copies = [
        remote(ct_in.at[0, k], wsib.at[k], w_sem, (k,), sibling(k)) for k in range(levels - 1)
    ]
    for copy in w_copies:
        copy.start()

    for copy in early:
        copy.wait()
    places = lax.broadcasted_iota(jnp.int32, (rows, rows), 0)
    for l in range(leaves):
        position = order[l : l + 1, :] - py * rows
        onehot[l] = jnp.where(places == position, 1.0, 0.0).astype(BF16)
        inward = dot(onehot[l], bin_[l]).astype(BF16)
        values = dot_tn(rs[l], inward)
        for q in range(npy):
            coef[q, l] = values[q * n : (q + 1) * n]

    near_copies = {}
    for d in list(range(1, nx)) + [0]:
        copy = remote(coef.at[2 * chip(d) + 1 - c], near_in.at[d], near_sem, (d,), twin)
        copy.start()
        near_copies[d] = copy

    own_copies = []
    x_copies = {}
    step = rows // CHUNKS

    def x_copy(l, h, d):
        piece = pl.ds(h * step, step)
        return remote(
            g.at[0, 0, l, piece], g.at[0, d, l, piece], x_sem, (l, h, d - 1), peer(d)
        )

    for l in range(leaves):
        g[0, 0, l] = dot_tn(onehot[l], rs[l]).astype(BF16)
        copy = remote(g.at[0, 0, l], g.at[1, 0, l], own_sem, (l,), twin)
        copy.start()
        own_copies.append(copy)
        if l == 0:
            for d in range(1, nx):
                x_copies[0, 0, d] = x_copy(0, 0, d)
                x_copies[0, 0, d].start()

    far_copies = []
    for d in range(1, nx):
        near_copies[d].wait_recv()
        part[d] = coef[2 * chip(d) + c] + near_in[d]
        copy = remote(part.at[d], far_in.at[d], far_sem, (d,), peer(d))
        copy.start()
        far_copies.append(copy)
    near_copies[0].wait_recv()
    part[0] = coef[2 * x + c] + near_in[0]

    def multiply(l, side, d, first=False):
        q = 2 * chip(-d) + (c if side == 0 else 1 - c)
        product = dot(moved[l, q], g[side, d, l])
        near[l] = product if first else near[l] + product

    bout_load.wait()
    for l in range(leaves):
        bmoved[l] = dot(onehot[l], bout[l]).astype(BF16)
        for copy in dense_loads[l]:
            copy.wait()

        def move(q, carry, l=l):
            moved[l, q] = dot(onehot[l], dense[l, q]).astype(BF16)
            return carry

        lax.fori_loop(0, npy, move, 0)
        multiply(l, 0, 0, first=True)

    for copy in far_copies:
        copy.wait_send()
    for l in range(leaves):
        for h in range(CHUNKS):
            for d in range(1, nx):
                if (l, h, d) not in x_copies:
                    x_copies[l, h, d] = x_copy(l, h, d)
                    x_copies[l, h, d].start()

    total = part[0]
    for copy, d in zip(far_copies, range(1, nx)):
        copy.wait_recv()
        total = total + far_in[d]
    first_coef, second_coef = total[0], total[1]

    forwards = []

    def forward(l, h):
        piece = pl.ds(h * step, step)
        for d in range(1, nx):
            x_copies[l, h, d].wait_recv()
            copy = remote(
                g.at[0, d, l, piece], g.at[1, d, l, piece], fwd_sem, (l, h, d - 1), twin
            )
            copy.start()
            forwards.append(copy)

    for copy in tree_loads:
        copy.wait()
    subtree = lift(first_coef, lt[0]) + lift(second_coef, lt[1])
    coupled = []
    s_copies = []
    for k in range(levels):
        ssend[k] = subtree
        copy = remote(ssend.at[k], srecv.at[k], s_sem, (k,), sibling(k))
        copy.start()
        s_copies.append(copy)
        if k == 0:
            first_down = lower(second_coef, lc[0])
            second_down = lower(first_coef, lc[1])
        else:
            coupled.append(lower(srecv[k - 1], cc[0, k - 1]))
        if k < levels - 1:
            own = lift(subtree, ct[0, k])
        if k == 0:
            for l in range(leaves):
                own_copies[l].wait_recv()
                multiply(l, 1, 0)
        if k == levels - 1:
            forward(0, 0)
            forward(0, 1)
        copy.wait_recv()
        if k < levels - 1:
            w_copies[k].wait_recv()
            subtree = own + lift(srecv[k], wsib[k])

    descend = lower(srecv[levels - 1], cc[0, levels - 1])
    for k in reversed(range(levels - 1)):
        descend = coupled[k] + lower(descend, ct[0, k])
    ldg[py, 0] = (first_down + lower(descend, lt[0])).astype(BF16)
    ldg[py, 1] = (second_down + lower(descend, lt[1])).astype(BF16)

    ld_copies = []
    for d in range(1, nx):
        ld_copies.append(remote(ldg.at[py], ldg.at[py], ld_sem, (d,), peer(d)))
    ld_twin = remote(ldg.at[py], ldg.at[py], ld_sem, (0,), twin)
    for copy in ld_copies + [ld_twin]:
        copy.start()

    for l in range(leaves):
        for h in range(CHUNKS):
            if l > 0 or h > 1:
                forward(l, h)
        if l == 0:
            for d in range(1, nx):
                multiply(0, 0, d)

    ld_forwards = []
    for d in range(1, nx):
        ld_copies[d - 1].wait_recv()
        block = ldg.at[2 * chip(-d) + c]
        copy = remote(block, block, ldf_sem, (d - 1,), twin)
        copy.start()
        ld_forwards.append(copy)
    for d in range(1, nx):
        multiply(1, 0, d)

    per_leaf = (nx - 1) * CHUNKS
    for copy in forwards[:per_leaf]:
        copy.wait_recv()
    for d in range(1, nx):
        multiply(0, 1, d)
    for copy in forwards[per_leaf:]:
        copy.wait_recv()
    for d in range(1, nx):
        multiply(1, 1, d)
    ld_twin.wait_recv()
    for copy in ld_forwards:
        copy.wait_recv()
    out_copies = []
    for l in range(leaves):
        down = ldg[:, l].reshape(width, ldg.shape[3])
        result[l] = near[l] + dot_nt(bmoved[l], down)
        copy = pltpu.make_async_copy(result.at[l], out.at[l], out_sem.at[l])
        copy.start()
        out_copies.append(copy)

    for copy in list(near_copies.values()) + own_copies + list(x_copies.values()):
        copy.wait_send()
    for copy in w_copies + forwards + s_copies + ld_copies + [ld_twin] + ld_forwards:
        copy.wait_send()
    for copy in out_copies:
        copy.wait()


def on_device(
    right_sides,
    tree_order,
    dense_blocks,
    basis_out,
    basis_in,
    leaf_transfer,
    leaf_coupling,
    chain_transfer,
    chain_coupling,
):
    npx = lax.axis_size("px")
    npy = lax.axis_size("py")
    levels = npx.bit_length() - 1
    nx = npy // 2
    leaves, rows, width = right_sides.shape
    rank = basis_in.shape[2]
    n = width // npy
    dma = pltpu.SemaphoreType.DMA
    anywhere = pl.BlockSpec(memory_space=pl.ANY)
    inside = pl.BlockSpec(memory_space=pltpu.VMEM)
    scratch = [
        pltpu.VMEM((leaves, rows, width), BF16),
        pltpu.VMEM((leaves, npy, rows, rows), BF16),
        pltpu.VMEM((leaves, rows, rank), BF16),
        pltpu.VMEM((leaves, rows, rank), BF16),
        pltpu.VMEM(leaf_transfer.shape, BF16),
        pltpu.VMEM(leaf_coupling.shape, BF16),
        pltpu.VMEM(chain_transfer.shape, BF16),
        pltpu.VMEM(chain_coupling.shape, BF16),
        pltpu.VMEM((leaves, rows, rows), BF16),
        pltpu.VMEM((leaves, npy, rows, rows), BF16),
        pltpu.VMEM((leaves, rows, rank), BF16),
        pltpu.VMEM((npy, leaves, n, rank), F32),
        pltpu.VMEM((nx, leaves, n, rank), F32),
        pltpu.VMEM((nx, leaves, n, rank), F32),
        pltpu.VMEM((nx, leaves, n, rank), F32),
        pltpu.VMEM((2, nx, leaves, rows, width), BF16),
        pltpu.VMEM((leaves, rows, width), F32),
        pltpu.VMEM((levels - 1, rank, rank), BF16),
        pltpu.VMEM((levels, n, rank), F32),
        pltpu.VMEM((levels, n, rank), F32),
        pltpu.VMEM((npy, leaves, n, rank), BF16),
        pltpu.VMEM((leaves, rows, width), F32),
        dma((7 + leaves * npy,)),
        dma((leaves,)),
        dma((2, levels - 1)),
        dma((2, nx)),
        dma((2, nx)),
        dma((2, leaves)),
        dma((2, leaves, CHUNKS, nx - 1)),
        dma((2, leaves, CHUNKS, nx - 1)),
        dma((2, levels)),
        dma((2, nx)),
        dma((2, nx - 1)),
    ]
    return pl.pallas_call(
        functools.partial(kernel, npx, npy),
        out_shape=jax.ShapeDtypeStruct((leaves, rows, width), F32),
        in_specs=[anywhere, inside] + [anywhere] * 7,
        out_specs=anywhere,
        scratch_shapes=scratch,
        compiler_params=pltpu.CompilerParams(
            collective_id=0, has_side_effects=True, vmem_limit_bytes=48 * 2**20
        ),
    )(
        right_sides,
        tree_order,
        dense_blocks,
        basis_out,
        basis_in,
        leaf_transfer,
        leaf_coupling,
        chain_transfer,
        chain_coupling,
    )


def solution(mesh):
    in_specs = (
        P("px", "py", None),
        P("px", "py"),
        P("px", "py", None),
        P("px", "py", None),
        P("px", "py", None),
        P("px", None, None),
        P("px", None, None),
        P("px", None, None, None),
        P("px", None, None, None),
    )
    out_specs = P("px", "py", None)
    return jax.shard_map(
        on_device, mesh=mesh, in_specs=in_specs, out_specs=out_specs, check_vma=False
    )
```

time: 134 us -> 51.2 us (0.38)
  waiting for transfers between devices: 80.8 us -> 0 us
  Pallas kernels: 0 us -> 41.5 us
  matrix products: 16.3 us -> 0 us
  between operations: 13.6 us -> 0.02 us
  starting transfers between devices: 7.88 us -> 0 us
  local copies, waits for them, and re-layouts: 14 us -> 9.2 us
    ppermute x5 -> x0, waiting for transfers between devices: 42 us -> none  [partner(): return lax.ppermute(value, axis, pairs)]
    pallas_call x0 -> x1, Pallas kernels: none -> 41.5 us  [on_device(): pl.pallas_call(functools.partial(kernel, npx, npy), out_shape=jax.ShapeDt...]
    psum x1 -> x0, waiting for transfers between devices: 38.1 us -> none  [on_device(): coefficients = lax.psum(coefficients, 'py')]
    dot_general x17 -> x0, matrix products: 16.3 us -> none  [the longest x1 5.85 us: on_device(): jnp.einsum('npk,nkr->npr', dense_blocks, lax.all_gather(permuted, 'py', a...]
    ppermute x5 -> x0, starting transfers between devices: 7.84 us -> none  [partner(): return lax.ppermute(value, axis, pairs)]
    gather x1 -> x0, local copies, waits for them, and re-layouts: 7.29 us -> none  [pick_rows(): return values[indices]]
    unnamed x27 -> x17, local copies, waits for them, and re-layouts: 6.72 us -> 9.2 us
  transfers between devices with their start and end apart: 7 -> 0, of which waited for: 5 -> 0; matrix products, arithmetic and copies ran while one was open for 7% -> 0% of each run, Pallas kernels for 0% -> 0%
where the time goes in v1:
time: 51.2 us; the launch traced here: 50.7 us
  Pallas kernels  41.5 us (81%)
  local copies, waits for them, and re-layouts  9.2 us (18%)
    pallas_call x1, Pallas kernels, on_device(): pl.pallas_call(functools.partial(kernel, npx, npy), out_shape=jax.ShapeDt...  41.5 us
    unnamed x17, local copies, waits for them, and re-layouts  9.2 us

profile of v1, /device:TPU:0, one launch (start us, length us, event | category | flops | bytes accessed | tf_op | source)
XLA Modules:
  0.0 50.7 jit_solution(14838742145765112629)
XLA Ops:
  0.0 0.0 copy-start
  0.0 1.2 %copy-done = bf16[2,512,512]{2,1,0:T(8,128)(2,1)S(1)} copy-done((bf16[2,512,512]{2,1,0:T(8,128)(2,1)S(1)}, bf16[2,512,512]{2,1,0:T(8,128)(2,1)}, u32[]{:S(2)}) %copy-start) | copy-done | bytes 1048600
  1.2 0.0 copy-start.1
  1.2 1.0 %copy-done.1 = bf16[2,512,256]{2,1,0:T(8,128)(2,1)S(1)} copy-done((bf16[2,512,256]{2,1,0:T(8,128)(2,1)S(1)}, bf16[2,512,256]{2,1,0:T(8,128)(2,1)}, u32[]{:S(2)}) %copy-start.1) | copy-done | bytes 524312
  2.3 0.0 copy-start.2
  2.3 1.0 %copy-done.2 = bf16[2,512,256]{2,1,0:T(8,128)(2,1)S(1)} copy-done((bf16[2,512,256]{2,1,0:T(8,128)(2,1)S(1)}, bf16[2,512,256]{2,1,0:T(8,128)(2,1)}, u32[]{:S(2)}) %copy-start.2) | copy-done | bytes 524312
  3.3 0.0 copy-start.3
  3.3 1.0 %copy-done.3 = bf16[1,3,256,256]{3,2,1,0:T(8,128)(2,1)S(1)} copy-done((bf16[1,3,256,256]{3,2,1,0:T(8,128)(2,1)S(1)}, bf16[1,3,256,256]{3,2,1,0:T(8,128)(2,1)}, u32[]{:S(2)}) %copy-start.3) | copy-done | bytes 393240
  4.3 0.0 copy-start.4
  4.3 1.0 %copy-done.4 = bf16[1,3,256,256]{3,2,1,0:T(8,128)(2,1)S(1)} copy-done((bf16[1,3,256,256]{3,2,1,0:T(8,128)(2,1)S(1)}, bf16[1,3,256,256]{3,2,1,0:T(8,128)(2,1)}, u32[]{:S(2)}) %copy-start.4) | copy-done | bytes 393240
  5.3 0.0 copy-start.5
  5.3 0.9 %copy-done.5 = bf16[2,256,256]{2,1,0:T(8,128)(2,1)S(1)} copy-done((bf16[2,256,256]{2,1,0:T(8,128)(2,1)S(1)}, bf16[2,256,256]{2,1,0:T(8,128)(2,1)}, u32[]{:S(2)}) %copy-start.5) | copy-done | bytes 262168
  6.3 0.0 copy-start.6
  6.3 0.9 %copy-done.6 = bf16[2,256,256]{2,1,0:T(8,128)(2,1)S(1)} copy-done((bf16[2,256,256]{2,1,0:T(8,128)(2,1)S(1)}, bf16[2,256,256]{2,1,0:T(8,128)(2,1)}, u32[]{:S(2)}) %copy-start.6) | copy-done | bytes 262168
  7.2 0.0 copy-start.7
  7.2 0.7 %copy-done.7 = s32[2,512]{1,0:T(2,128)S(1)} copy-done((s32[2,512]{1,0:T(2,128)S(1)}, s32[2,512]{1,0:T(2,128)}, u32[]{:S(2)}) %copy-start.7) | copy-done | bytes 4120
  7.9 41.5 %shard_map.91 = f32[2,512,512]{2,1,0:T(8,128)S(1)} custom-call(bf16[2,512,512]{2,1,0:T(8,128)(2,1)S(1)} %copy-done, s32[2,512]{1,0:T(2,128)S(1)} %copy-done.7, bf16[2,512,2048]{2,1,0:T(8,128)(2,1)} %dense_in.1, bf16[2,512,256]{2,1,0:T(8,128)(2,1)S(1)} %copy-done.1, bf16[2,512,256]{2,1,0:T(8,128)(2,1)S(1)} %copy-done.2, bf16[2,256,256]{2,1,0:T(8,128)(2,1)S(1)} %copy-done.5, ...), custom_call_target="tpu_custom_call" | custom-call | tf_op jit(solution)/shard_map/pallas_call | solution.py:387
  49.4 1.3 %copy.11 = f32[2,512,512]{2,1,0:T(8,128)} copy(f32[2,512,512]{2,1,0:T(8,128)S(1)} %shard_map.91) | data formatting | bytes 4194304
Async XLA Ops:
  0.0 1.2 %copy-start = (bf16[2,512,512]{2,1,0:T(8,128)(2,1)S(1)}, bf16[2,512,512]{2,1,0:T(8,128)(2,1)}, u32[]{:S(2)}) copy-start(bf16[2,512,512]{2,1,0:T(8,128)(2,1)} %rs_in.1) | copy-start | bytes 3145732
  1.2 1.0 %copy-start.1 = (bf16[2,512,256]{2,1,0:T(8,128)(2,1)S(1)}, bf16[2,512,256]{2,1,0:T(8,128)(2,1)}, u32[]{:S(2)}) copy-start(bf16[2,512,256]{2,1,0:T(8,128)(2,1)} %bout_in.1) | copy-start | bytes 1572868
  2.3 1.0 %copy-start.2 = (bf16[2,512,256]{2,1,0:T(8,128)(2,1)S(1)}, bf16[2,512,256]{2,1,0:T(8,128)(2,1)}, u32[]{:S(2)}) copy-start(bf16[2,512,256]{2,1,0:T(8,128)(2,1)} %bin_in.1) | copy-start | bytes 1572868
  3.3 1.0 %copy-start.3 = (bf16[1,3,256,256]{3,2,1,0:T(8,128)(2,1)S(1)}, bf16[1,3,256,256]{3,2,1,0:T(8,128)(2,1)}, u32[]{:S(2)}) copy-start(bf16[1,3,256,256]{3,2,1,0:T(8,128)(2,1)} %ct_in.1) | copy-start | bytes 1179652
  4.3 1.0 %copy-start.4 = (bf16[1,3,256,256]{3,2,1,0:T(8,128)(2,1)S(1)}, bf16[1,3,256,256]{3,2,1,0:T(8,128)(2,1)}, u32[]{:S(2)}) copy-start(bf16[1,3,256,256]{3,2,1,0:T(8,128)(2,1)} %cc_in.1) | copy-start | bytes 1179652
  5.3 0.9 %copy-start.5 = (bf16[2,256,256]{2,1,0:T(8,128)(2,1)S(1)}, bf16[2,256,256]{2,1,0:T(8,128)(2,1)}, u32[]{:S(2)}) copy-start(bf16[2,256,256]{2,1,0:T(8,128)(2,1)} %lt_in.1) | copy-start | bytes 786436
  6.3 0.9 %copy-start.6 = (bf16[2,256,256]{2,1,0:T(8,128)(2,1)S(1)}, bf16[2,256,256]{2,1,0:T(8,128)(2,1)}, u32[]{:S(2)}) copy-start(bf16[2,256,256]{2,1,0:T(8,128)(2,1)} %lc_in.1) | copy-start | bytes 786436
  7.2 0.7 %copy-start.7 = (s32[2,512]{1,0:T(2,128)S(1)}, s32[2,512]{1,0:T(2,128)}, u32[]{:S(2)}) copy-start(s32[2,512]{1,0:T(2,128)} %order.1) | copy-start | bytes 12292

commit v2 on v1

v2 whole, which is shorter than its diff:
```python
import functools

import jax
import jax.numpy as jnp
from jax import lax
from jax.experimental import pallas as pl
from jax.experimental.pallas import tpu as pltpu
from jax.sharding import PartitionSpec as P

MESH = pl.DeviceIdType.MESH
BF16 = jnp.bfloat16
F32 = jnp.float32
CHUNKS = 4
FIRST, SECOND, THIRD = 1, 4, 7
PARTS = 2
VMEM = 58 * 2**20


def dot(a, b):
    return jnp.dot(a, b, preferred_element_type=F32)


def dot_nt(a, b):
    return lax.dot_general(a, b, (((1,), (1,)), ((), ())), preferred_element_type=F32)


def dot_tn(a, b):
    return lax.dot_general(a, b, (((0,), (0,)), ((), ())), preferred_element_type=F32)


def halves(v):
    high = v.astype(BF16)
    low = (v - high.astype(F32)).astype(BF16)
    return jnp.concatenate([high, low], axis=0)


def lift(v, w):
    t = dot(halves(v), w)
    n = v.shape[0]
    return t[:n] + t[n:]


def lower(v, w):
    t = dot_nt(halves(v), w)
    n = v.shape[0]
    return t[:n] + t[n:]


def kernel(
    npx,
    npy,
    rs_in,
    order_in,
    dense_in,
    bout_in,
    bin_in,
    lt_in,
    lc_in,
    ct_in,
    cc_in,
    out,
    orders,
    dense,
    bout,
    bin_,
    lt,
    lc,
    ct,
    cc,
    onehot,
    moved,
    bmoved,
    coef,
    near_in,
    part,
    far_in,
    g,
    near,
    wsib,
    ssend,
    srecv,
    ldg,
    load_sem,
    out_sem,
    order_sem,
    w_sem,
    near_sem,
    far_sem,
    own_sem,
    x_sem,
    fwd_sem,
    s_sem,
    ld_sem,
    ldf_sem,
):
    levels = npx.bit_length() - 1
    nx = npy // 2
    leaves, rows, width = rs_in.shape
    n = width // npy
    px = lax.axis_index("px")
    py = lax.axis_index("py")
    x = py // 2
    c = py % 2
    twin = {"py": 2 * x + 1 - c}

    def chip(d):
        return lax.rem(x + d + nx, nx)

    def peer(d):
        return {"py": 2 * chip(d) + c}

    def sibling(k):
        bit = (px // 2**k) % 2
        return {"px": px + 2**k * (1 - 2 * bit)}

    def remote(src, dst, sems, index, device):
        return pltpu.make_async_remote_copy(
            src_ref=src,
            dst_ref=dst,
            send_sem=sems.at[(0,) + index],
            recv_sem=sems.at[(1,) + index],
            device_id=device,
            device_id_type=MESH,
        )

    loads = []
    sent = []

    def load(src, dst):
        copy = pltpu.make_async_copy(src, dst, load_sem.at[len(loads)])
        copy.start()
        loads.append(copy)
        return copy

    def send(*args):
        copy = remote(*args)
        copy.start()
        sent.append(copy)
        return copy

    order_load = load(order_in, orders.at[py])
    early = [load(bin_in, bin_), load(rs_in, g.at[0, 0])]
    tree_loads = [load(lt_in, lt), load(ct_in, ct), load(lc_in, lc), load(cc_in, cc)]
    bout_load = load(bout_in, bout)
    dense_loads = [
        [load(dense_in.at[l, :, pl.ds(q * rows, rows)], dense.at[l, q]) for q in range(npy)]
        for l in range(leaves)
    ]

    others = [{"py": lax.rem(py + d, npy)} for d in range(1, npy)]
    partners = others + [sibling(k) for k in range(levels)]
    barrier = pltpu.get_barrier_semaphore()
    for device in partners:
        pl.semaphore_signal(barrier, inc=1, device_id=device, device_id_type=MESH)

    places = lax.broadcasted_iota(jnp.int32, (rows, rows), 0)

    def selection(l, q):
        position = orders[q, pl.ds(l, 1), :] - q * rows
        return jnp.where(places == position, 1.0, 0.0).astype(BF16)

    order_load.wait()
    for l in range(leaves):
        onehot[l] = selection(l, py)
    pl.semaphore_wait(barrier, len(partners))

    step = rows // CHUNKS
    pieces = [(l, h) for l in range(leaves) for h in range(CHUNKS)]
    x_copies = {}

    def spread(wanted):
        for l, h in wanted:
            piece = pl.ds(h * step, step)
            for d in range(1, nx):
                x_copies[l, h, d] = send(
                    rs_in.at[l, piece], g.at[0, d, l, piece], x_sem, (l, h, d - 1), peer(d)
                )

    spread(pieces[:FIRST])
    order_copies = [
        send(orders.at[py], orders.at[py], order_sem, (d,), device)
        for d, device in enumerate(others)
    ]
    w_copies = [
        send(ct_in.at[0, k], wsib.at[k], w_sem, (k,), sibling(k)) for k in range(levels - 1)
    ]

    near_copies = {}
    for copy in early:
        copy.wait()
    for l in range(leaves):
        inward = dot(onehot[l], bin_[l]).astype(BF16)
        values = dot_tn(g[0, 0, l], inward)
        for q in range(npy):
            coef[q, l] = values[q * n : (q + 1) * n]
        for d in list(range(1, nx)) + [0]:
            near_copies[l, d] = send(
                coef.at[2 * chip(d) + 1 - c, l], near_in.at[d, l], near_sem, (l, d), twin
            )
    own_copies = [
        send(rs_in.at[l], g.at[1, 0, l], own_sem, (l,), twin) for l in range(leaves)
    ]

    half = n // PARTS
    spans = [pl.ds(t * half, half) for t in range(PARTS)]
    far_copies = {}
    for l in range(leaves):
        for d in range(1, nx):
            near_copies[l, d].wait_recv()
            q = 2 * chip(d) + c
            part[d, l] = coef[q, l] + near_in[d, l]
            for t in range(PARTS):
                far_copies[l, t, d] = send(
                    part.at[d, l, spans[t]],
                    far_in.at[d, l, spans[t]],
                    far_sem,
                    (l, t, d),
                    peer(d),
                )
    for l in range(leaves):
        near_copies[l, 0].wait_recv()
        part[0, l] = coef[2 * x + c, l] + near_in[0, l]

    def owner(side, d):
        return 2 * chip(-d) + (c if side == 0 else 1 - c)

    def move(l, q):
        turned = dot(onehot[l], dense[l, q]).astype(BF16)
        moved[l, q] = dot_nt(turned, selection(l, q)).astype(BF16)

    def multiply(l, side, d, first=False):
        product = dot(moved[l, owner(side, d)], g[side, d, l])
        near[l] = product if first else near[l] + product

    def multiply_piece(l, side, d, start, stop):
        q = owner(side, d)
        piece = slice(start * step, stop * step)
        return dot(moved[l, q, :, piece], g[side, d, l, piece])

    for copy in order_copies:
        copy.wait_recv()
    for l in range(leaves):
        for copy in dense_loads[l]:
            copy.wait()

    def move_some(start, stop):
        def one(i, carry):
            move(lax.div(i, npy), lax.rem(i, npy))
            return carry

        lax.fori_loop(start, stop, one, 0)

    out_copies = []
    units = leaves * npy
    marks = [units * m // 8 for m in (0, 5, 6, 7, 8)]
    bout_load.wait()
    for l in range(leaves):
        bmoved[l] = dot(onehot[l], bout[l]).astype(BF16)

    move_some(marks[0], marks[1])
    for copy in far_copies.values():
        copy.wait_send()
    spread(pieces[FIRST:SECOND])

    forwards = []

    def forward(l, h):
        piece = pl.ds(h * step, step)
        for d in range(1, nx):
            x_copies[l, h, d].wait_recv()
            forwards.append(
                send(g.at[0, d, l, piece], g.at[1, d, l, piece], fwd_sem, (l, h, d - 1), twin)
            )

    for copy in tree_loads:
        copy.wait()
    s_copies = {}
    coefs = []
    own = {}
    for t in range(PARTS):
        total = part[0, :, spans[t]]
        for d in range(1, nx):
            for l in range(leaves):
                far_copies[l, t, d].wait_recv()
            total = total + far_in[d, :, spans[t]]
        coefs.append(total)
        ssend[0, spans[t]] = lift(total[0], lt[0]) + lift(total[1], lt[1])
        s_copies[0, t] = send(
            ssend.at[0, spans[t]], srecv.at[0, spans[t]], s_sem, (0, t), sibling(0)
        )
    first_down, second_down, coupled = [], [], {}
    for k in range(levels):
        if k < levels - 1:
            for t in range(PARTS):
                own[t] = lift(ssend[k, spans[t]], ct[0, k])
        if k == 0:
            for t in range(PARTS):
                first_down.append(lower(coefs[t][1], lc[0]))
                second_down.append(lower(coefs[t][0], lc[1]))
        if k == 1:
            spread(pieces[SECOND:THIRD])
        if k < 3:
            move_some(marks[k + 1], marks[k + 2])
        if k < levels - 1:
            w_copies[k].wait_recv()
            for t in range(PARTS):
                s_copies[k, t].wait_recv()
                ssend[k + 1, spans[t]] = own[t] + lift(srecv[k, spans[t]], wsib[k])
                s_copies[k + 1, t] = send(
                    ssend.at[k + 1, spans[t]],
                    srecv.at[k + 1, spans[t]],
                    s_sem,
                    (k + 1, t),
                    sibling(k + 1),
                )
            for t in range(PARTS):
                coupled[k, t] = lower(srecv[k, spans[t]], cc[0, k])
    for l, h in pieces[:FIRST]:
        forward(l, h)
    for l in range(leaves):
        own_copies[l].wait_recv()
        multiply(l, 0, 0, first=True)
        multiply(l, 1, 0)

    ld_copies = {}
    ld_twin = {}
    top = levels - 1
    for t in range(PARTS):
        s_copies[top, t].wait_recv()
        descend = lower(srecv[top, spans[t]], cc[0, top])
        for k in reversed(range(top)):
            descend = coupled[k, t] + lower(descend, ct[0, k])
        ldg[py, 0, spans[t]] = (first_down[t] + lower(descend, lt[0])).astype(BF16)
        ldg[py, 1, spans[t]] = (second_down[t] + lower(descend, lt[1])).astype(BF16)
        block = ldg.at[py, :, spans[t]]
        for d in range(1, nx):
            ld_copies[t, d] = send(block, block, ld_sem, (t, d), peer(d))
        ld_twin[t] = send(block, block, ld_sem, (t, 0), twin)
    spread(pieces[THIRD:])

    for l, h in pieces[FIRST:THIRD]:
        forward(l, h)
    for d in range(1, nx):
        multiply(0, 0, d)
    for copy in forwards[: (nx - 1) * CHUNKS]:
        copy.wait_recv()
    for d in range(1, nx):
        multiply(0, 1, d)

    ld_forwards = []
    for t in range(PARTS):
        for d in range(1, nx):
            ld_copies[t, d].wait_recv()
            block = ldg.at[owner(0, d), :, spans[t]]
            ld_forwards.append(send(block, block, ldf_sem, (t, d - 1), twin))
    for l, h in pieces[THIRD:]:
        forward(l, h)
    for t in range(PARTS):
        ld_twin[t].wait_recv()
    for copy in ld_forwards:
        copy.wait_recv()
    last = leaves - 1
    half = CHUNKS // 2
    for l in range(leaves):
        near[l] += dot_nt(bmoved[l], ldg[:, l].reshape(width, ldg.shape[3]))
        if l < last:
            copy = pltpu.make_async_copy(near.at[l], out.at[l], out_sem.at[l])
            copy.start()
            out_copies.append(copy)
    for start, stop in ((0, half), (half, CHUNKS - 1), (CHUNKS - 1, CHUNKS)):
        first, end = (nx - 1) * (last * CHUNKS + start), (nx - 1) * (last * CHUNKS + stop)
        for copy in forwards[first:end]:
            copy.wait_recv()
        total = near[last]
        for d in range(1, nx):
            for side in range(2):
                total = total + multiply_piece(last, side, d, start, stop)
        near[last] = total
    copy = pltpu.make_async_copy(near.at[last], out.at[last], out_sem.at[last])
    copy.start()
    out_copies.append(copy)

    for copy in sent:
        if not any(copy is other for other in far_copies.values()):
            copy.wait_send()
    for copy in out_copies:
        copy.wait()


def on_device(
    right_sides,
    tree_order,
    dense_blocks,
    basis_out,
    basis_in,
    leaf_transfer,
    leaf_coupling,
    chain_transfer,
    chain_coupling,
):
    npx = lax.axis_size("px")
    npy = lax.axis_size("py")
    levels = npx.bit_length() - 1
    nx = npy // 2
    leaves, rows, width = right_sides.shape
    rank = basis_in.shape[2]
    n = width // npy
    dma = pltpu.SemaphoreType.DMA
    outside = pl.BlockSpec(memory_space=pltpu.HBM)
    scratch = [
        pltpu.VMEM((npy, leaves, rows), jnp.int32),
        pltpu.VMEM((leaves, npy, rows, rows), BF16),
        pltpu.VMEM((leaves, rows, rank), BF16),
        pltpu.VMEM((leaves, rows, rank), BF16),
        pltpu.VMEM(leaf_transfer.shape, BF16),
        pltpu.VMEM(leaf_coupling.shape, BF16),
        pltpu.VMEM(chain_transfer.shape, BF16),
        pltpu.VMEM(chain_coupling.shape, BF16),
        pltpu.VMEM((leaves, rows, rows), BF16),
        pltpu.VMEM((leaves, npy, rows, rows), BF16),
        pltpu.VMEM((leaves, rows, rank), BF16),
        pltpu.VMEM((npy, leaves, n, rank), F32),
        pltpu.VMEM((nx, leaves, n, rank), F32),
        pltpu.VMEM((nx, leaves, n, rank), F32),
        pltpu.VMEM((nx, leaves, n, rank), F32),
        pltpu.VMEM((2, nx, leaves, rows, width), BF16),
        pltpu.VMEM((leaves, rows, width), F32),
        pltpu.VMEM((levels - 1, rank, rank), BF16),
        pltpu.VMEM((levels, n, rank), F32),
        pltpu.VMEM((levels, n, rank), F32),
        pltpu.VMEM((npy, leaves, n, rank), BF16),
        dma((8 + leaves * npy,)),
        dma((leaves,)),
        dma((2, npy - 1)),
        dma((2, levels - 1)),
        dma((2, leaves, nx)),
        dma((2, leaves, PARTS, nx)),
        dma((2, leaves)),
        dma((2, leaves, CHUNKS, nx - 1)),
        dma((2, leaves, CHUNKS, nx - 1)),
        dma((2, levels, PARTS)),
        dma((2, PARTS, nx)),
        dma((2, PARTS, nx - 1)),
    ]
    return pl.pallas_call(
        functools.partial(kernel, npx, npy),
        out_shape=jax.ShapeDtypeStruct((leaves, rows, width), F32),
        in_specs=[outside] * 9,
        out_specs=outside,
        scratch_shapes=scratch,
        compiler_params=pltpu.CompilerParams(
            collective_id=0, has_side_effects=True, vmem_limit_bytes=VMEM
        ),
    )(
        right_sides,
        tree_order,
        dense_blocks,
        basis_out,
        basis_in,
        leaf_transfer,
        leaf_coupling,
        chain_transfer,
        chain_coupling,
    )


def solution(mesh):
    in_specs = (
        P("px", "py", None),
        P("px", "py"),
        P("px", "py", None),
        P("px", "py", None),
        P("px", "py", None),
        P("px", None, None),
        P("px", None, None),
        P("px", None, None, None),
        P("px", None, None, None),
    )
    out_specs = P("px", "py", None)
    return jax.shard_map(
        on_device, mesh=mesh, in_specs=in_specs, out_specs=out_specs, check_vma=False
    )
```

time: 51.2 us -> 44.7 us (0.87)
  local copies, waits for them, and re-layouts: 9.2 us -> 3.08 us
    unnamed x17 -> x1, local copies, waits for them, and re-layouts: 9.2 us -> 3.08 us
where the time goes in v2:
time: 44.7 us; the launch traced here: 44.6 us
  Pallas kernels  41.5 us (93%)
  local copies, waits for them, and re-layouts  3.08 us (7%)
    pallas_call x1, Pallas kernels, on_device(): pl.pallas_call(functools.partial(kernel, npx, npy), out_shape=jax.ShapeDt...  41.5 us
    unnamed x1, local copies, waits for them, and re-layouts  3.08 us

profile of v2, /device:TPU:0, one launch (start us, length us, event | category | flops | bytes accessed | tf_op | source)
XLA Modules:
  0.0 44.6 jit_solution(12013502568725457156)
XLA Ops:
  0.0 41.5 %shard_map.91 = f32[2,512,512]{2,1,0:T(8,128)} custom-call(bf16[2,512,512]{2,1,0:T(8,128)(2,1)} %rs_in.1, s32[2,512]{1,0:T(2,128)} %order_in.1, bf16[2,512,2048]{2,1,0:T(8,128)(2,1)} %dense_in.1, bf16[2,512,256]{2,1,0:T(8,128)(2,1)} %bout_in.1, bf16[2,512,256]{2,1,0:T(8,128)(2,1)} %bin_in.1, bf16[2,256,256]{2,1,0:T(8,128)(2,1)} %lt_in.1, ...), custom_call_target="tpu_custom_call" | custom-call | tf_op jit(solution)/shard_map/pallas_call | solution.py:445
  41.5 3.1 %copy.11 = f32[2,512,512]{2,1,0:T(8,128)} copy(f32[2,512,512]{2,1,0:T(8,128)} %shard_map.91) | data formatting | bytes 4194304

commit v3 on v2

--- a/solution.py
+++ b/solution.py
@@ -11,7 +11,7 @@
 BF16 = jnp.bfloat16
 F32 = jnp.float32
 CHUNKS = 4
-FIRST, SECOND, THIRD = 1, 4, 7
+FIRST, SECOND, THIRD = 1, 5, 7
 PARTS = 2
 VMEM = 58 * 2**20
 
@@ -257,10 +257,11 @@
     for l in range(leaves):
         bmoved[l] = dot(onehot[l], bout[l]).astype(BF16)
 
-    move_some(marks[0], marks[1])
+    move_some(marks[0], marks[0] + units // 4)
     for copy in far_copies.values():
         copy.wait_send()
     spread(pieces[FIRST:SECOND])
+    move_some(marks[0] + units // 4, marks[1])
 
     forwards = []
 

time: 44.7 us -> 44.1 us (0.987)
  Pallas kernels: 41.5 us -> 40.8 us
    pallas_call x1, Pallas kernels: 41.5 us -> 40.8 us  [on_device(): pl.pallas_call(functools.partial(kernel, npx, npy), out_shape=jax.ShapeDt...]
where the time goes in v3:
time: 44.1 us; the launch traced here: 43.9 us
  Pallas kernels  40.8 us (93%)
  local copies, waits for them, and re-layouts  3.08 us (7%)
    pallas_call x1, Pallas kernels, on_device(): pl.pallas_call(functools.partial(kernel, npx, npy), out_shape=jax.ShapeDt...  40.8 us
    unnamed x1, local copies, waits for them, and re-layouts  3.08 us

profile of v3, /device:TPU:0, one launch (start us, length us, event | category | flops | bytes accessed | tf_op | source)
XLA Modules:
  0.0 43.9 jit_solution(9569612368510702901)
XLA Ops:
  0.0 40.8 %shard_map.91 = f32[2,512,512]{2,1,0:T(8,128)} custom-call(bf16[2,512,512]{2,1,0:T(8,128)(2,1)} %rs_in.1, s32[2,512]{1,0:T(2,128)} %order_in.1, bf16[2,512,2048]{2,1,0:T(8,128)(2,1)} %dense_in.1, bf16[2,512,256]{2,1,0:T(8,128)(2,1)} %bout_in.1, bf16[2,512,256]{2,1,0:T(8,128)(2,1)} %bin_in.1, bf16[2,256,256]{2,1,0:T(8,128)(2,1)} %lt_in.1, ...), custom_call_target="tpu_custom_call" | custom-call | tf_op jit(solution)/shard_map/pallas_call | solution.py:446
  40.8 3.1 %copy.11 = f32[2,512,512]{2,1,0:T(8,128)} copy(f32[2,512,512]{2,1,0:T(8,128)} %shard_map.91) | data formatting | bytes 4194304
